TPU v7x, 32 devices: a whole 2x2x4 slice. The times are simulated.
32 devices in a mesh: doc: 8 (over z, y), head: 4 (over x, core).
Axes of the slice: x: 2, y: 2, z: 4, core: 2. Of those that a mesh axis runs over, the one named last changes fastest.
Arguments:
- target_q: bfloat16 [1024, 2048], P('doc', 'head'), may hold values from -300 to 300
- target_kv: bfloat16 [1024, 512], P('doc', 'head'), may hold values from -8 to 8
- doc_kv: bfloat16 [8, 384, 512], P('doc', None, 'head'), may hold values from -6 to 6
- doc_lengths: int32 [8], replicated, may hold values from 1 to 384, 2304 in all
- segment_ids: int32 [1024], replicated, may hold values from 0 to 15, never falling along the last dimension, each value on 1 to 128 neighbouring positions
- out_weight: bfloat16 [2048, 8192], P('head', 'doc'), may hold values from -0.125 to 0.125
Outputs:
- projected: bfloat16 [1024, 8192], P('head', 'doc')
Inputs may be any that keep to these rules, and one draw needn't show every extreme that they name: `segment_ids`: segment numbers never fall along the target rows, and each segment spans at most 128 rows.
All inputs are finite; a program needn't handle non-finite values.
Results may differ from a plain program's by a relative error of at most 0.005.
Values may be sent and summed in bfloat16 or wider, within the bound.
A program may use at most 64 MiB of HBM per device.

v0:
```python
import math
import jax
import jax.numpy as jnp
from jax import lax
from jax.sharding import PartitionSpec as P

masked_score = -1e30


def swapped(array, axis, stride):
    return lax.ppermute(array, axis, [(i, i ^ 1 << stride) for i in range(lax.axis_size(axis))])


def passed_along(value, axis, steps):
    count = lax.axis_size(axis)
    initial, last = (max(0, -steps), min(count, count - steps))
    return lax.ppermute(value, axis, [(source, source + steps) for source in range(initial, last)])


def block_stats(queries, key_block, value_block, visible):
    scaling = 1.0 / math.sqrt(key_block.shape[1])
    scores = (
        lax.dot_general(
            queries, key_block, (((1,), (1,)), ((), ())), preferred_element_type=jnp.float32
        )
        * scaling
    )
    scores = jnp.where(visible, scores, masked_score)
    highest = jnp.max(scores, axis=1)
    weights = jnp.exp(scores - highest[:, None])
    summed = jnp.sum(weights, axis=1)
    blended = jnp.dot(weights.astype(jnp.bfloat16), value_block, preferred_element_type=jnp.float32)
    return (highest, summed, blended)


def merge_stats(state_now, incoming):
    highest = jnp.maximum(state_now[0], incoming[0])
    old_factor = jnp.exp(state_now[0] - highest)
    new_factor = jnp.exp(incoming[0] - highest)
    summed = state_now[1] * old_factor + incoming[1] * new_factor
    blended = state_now[2] * old_factor[:, None] + incoming[2] * new_factor[:, None]
    return (highest, summed, blended)


def body(target_q, target_kv, doc_kv, doc_lengths, segment_ids, out_weight):
    row_count = target_q.shape[0]
    head_dim = target_kv.shape[1]
    per_device = target_q.shape[1] // head_dim
    queries = target_q.reshape(row_count * per_device, head_dim)
    parity = lax.axis_index("head") % 2
    doc_index = lax.axis_index("doc")

    def arrange(own_part, partner):
        return (
            jnp.where(parity == 0, own_part, partner),
            jnp.where(parity == 0, partner, own_part),
        )

    initial = (
        jnp.full((queries.shape[0],), masked_score, jnp.float32),
        jnp.zeros((queries.shape[0],), jnp.float32),
        jnp.zeros((queries.shape[0], head_dim), jnp.float32),
    )
    partner_doc, partner_tgt = swapped((doc_kv, target_kv), "head", 0)
    doc_keys, doc_values = arrange(doc_kv, partner_doc)
    key_docs = lax.all_gather(doc_keys, "doc", axis=0, tiled=True)
    value_docs = lax.all_gather(doc_values, "doc", axis=0, tiled=True)
    slot_index = jnp.arange(key_docs.shape[1], dtype=jnp.int32)

    def attend_doc(doc_step, running):
        key_block = lax.dynamic_index_in_dim(key_docs, doc_step, 0, keepdims=False)
        value_block = lax.dynamic_index_in_dim(value_docs, doc_step, 0, keepdims=False)
        length = lax.dynamic_index_in_dim(doc_lengths, doc_step, 0, keepdims=False)
        visible = (slot_index < length)[None, :]
        return merge_stats(running, block_stats(queries, key_block, value_block, visible))

    stats = lax.fori_loop(0, key_docs.shape[0], attend_doc, initial)
    own_keys, own_values = arrange(target_kv, partner_tgt)
    prev_keys, prev_values = passed_along((own_keys, own_values), "doc", 1)
    own_seg = lax.dynamic_slice_in_dim(segment_ids, doc_index * row_count, row_count)
    prev_start = jnp.maximum(doc_index - 1, 0) * row_count
    prev_seg = jnp.where(
        doc_index > 0, lax.dynamic_slice_in_dim(segment_ids, prev_start, row_count), -1
    )
    token_pos = jnp.arange(row_count, dtype=jnp.int32)
    own_mask = (own_seg[:, None] == own_seg[None, :]) & (token_pos[None, :] <= token_pos[:, None])
    prev_mask = own_seg[:, None] == prev_seg[None, :]
    stats = merge_stats(
        stats, block_stats(queries, own_keys, own_values, jnp.repeat(own_mask, per_device, axis=0))
    )
    stats = merge_stats(
        stats,
        block_stats(queries, prev_keys, prev_values, jnp.repeat(prev_mask, per_device, axis=0)),
    )
    attention = (
        (stats[2] / stats[1][:, None])
        .astype(jnp.bfloat16)
        .reshape(row_count, per_device * head_dim)
    )
    gathered = lax.all_gather(attention, "doc", axis=0, tiled=True)
    result = lax.psum_scatter(
        jnp.dot(gathered, out_weight, preferred_element_type=jnp.float32),
        "head",
        scatter_dimension=0,
        tiled=True,
    )
    return result.astype(jnp.bfloat16)


def solution(mesh):
    placed = (
        P("doc", "head"),
        P("doc", "head"),
        P("doc", None, "head"),
        P(),
        P(),
        P("head", "doc"),
    )
    return jax.shard_map(
        body, mesh=mesh, in_specs=placed, out_specs=P("head", "doc"), check_vma=False
    )
```

profile of v0, /device:TPU:0, one launch (start us, length us, event | category | flops | bytes accessed | tf_op | source)
XLA Modules:
  0.0 207.3 jit_solution(15352952914273228183)
XLA Ops:
  6.5 0.5 collective-permute-start.1
  7.1 0.8 fusion.38
  8.1 0.1 copy.9
  8.3 0.1 copy.10
  8.5 1.0 reshape.30
  9.5 1.4 broadcast_select_fusion.3
  10.9 4.9 %collective-permute-start.2 = (bf16[128,128]{1,0:T(8,128)(2,1)S(1)}, bf16[128,128]{1,0:T(8,128)(2,1)S(1)}, u32[]{:S(2)}, u32[]{:S(2)}) collective-permute-start(bf16[128,128]{1,0:T(8,128)(2,1)S(1)} %get-tuple-element.222), channel_id=1, source_target_pairs={{0,4},{4,8},{8,12},{12,16},{16,20},{20,24},{24,28},{1,5},{5,9},{9,... | collective-permute-start | bytes 98312 | tf_op jit(solution)/shard_map/ppermute | solution.py:17
  15.7 4.0 %collective-permute-start.3 = (bf16[128,128]{1,0:T(8,128)(2,1)}, bf16[128,128]{1,0:T(8,128)(2,1)}, u32[]{:S(2)}, u32[]{:S(2)}) collective-permute-start(bf16[128,128]{1,0:T(8,128)(2,1)} %get-tuple-element.223), channel_id=1, source_target_pairs={{0,4},{4,8},{8,12},{12,16},{16,20},{20,24},{24,28},{1,5},{5,9},{9,... | collective-permute-start | bytes 98312 | tf_op jit(solution)/shard_map/ppermute | solution.py:17
  19.8 0.2 fusion.40
  20.0 0.6 fusion.24
  20.6 0.2 fusion.39
  20.8 0.6 fusion.26
  21.5 0.9 broadcast_select_fusion
  22.4 32.1 %all_gather.10 = bf16[8,384,128]{2,1,0:T(8,128)(2,1)S(1)} all-gather(bf16[1,384,128]{2,1,0:T(8,128)(2,1)S(1)} %get-tuple-element.220), channel_id=1, replica_groups=mesh['doc'=8,'head'=4] {'doc'}, dimensions={0}, use_global_device_ids=true | all-gather | bytes 884736 | tf_op jit(solution)/shard_map/all_gather | solution.py:67
  54.5 32.1 %all_gather.9 = bf16[8,384,128]{2,1,0:T(8,128)(2,1)S(1)} all-gather(bf16[1,384,128]{2,1,0:T(8,128)(2,1)S(1)} %get-tuple-element.221), channel_id=1, replica_groups=mesh['doc'=8,'head'=4] {'doc'}, dimensions={0}, use_global_device_ids=true | all-gather | bytes 884736 | tf_op jit(solution)/shard_map/all_gather | solution.py:66
  86.7 21.7 %while.18 = (s32[]{:T(128)}, f32[512]{0:T(512)S(1)}, f32[512]{0:T(512)S(1)}, f32[512,128]{1,0:T(8,128)S(1)}, s32[8]{0:T(128)}, /*index=5*/bf16[8,384,128]{2,1,0:...) while((s32[]{:T(128)}, f32[512]{0:T(512)S(1)}, ...), condition=%wide.region_3.4_spmd.clone, body=%wide.region_0.3_spmd.clone.sunk | while | flops 102305152 | bytes 3240976 | solution.py:77
  86.7 1.2 dynamic_slice.51
  87.9 0.6 iota_compare_fusion.3
  88.5 0.3 fusion.61
  88.8 0.2 fusion.62
  88.9 0.4 fusion.64
  89.4 1.2 dynamic_slice.51
  90.6 0.6 iota_compare_fusion.3
  91.2 0.3 fusion.61
  91.5 0.2 fusion.62
  91.6 0.4 fusion.64
  92.1 1.2 dynamic_slice.51
  93.3 0.6 iota_compare_fusion.3
  93.9 0.3 fusion.61
  94.2 0.2 fusion.62
  94.3 0.4 fusion.64
  94.8 1.2 dynamic_slice.51
  96.0 0.6 iota_compare_fusion.3
  96.6 0.3 fusion.61
  96.9 0.2 fusion.62
  97.1 0.4 fusion.64
  97.5 1.2 dynamic_slice.51
  98.7 0.6 iota_compare_fusion.3
  99.3 0.3 fusion.61
  99.6 0.2 fusion.62
  99.8 0.4 fusion.64
  100.2 1.2 dynamic_slice.51
  101.4 0.6 iota_compare_fusion.3
  102.0 0.3 fusion.61
  102.3 0.2 fusion.62
  102.5 0.4 fusion.64
  102.9 1.2 dynamic_slice.51
  104.2 0.6 iota_compare_fusion.3
  104.7 0.3 fusion.61
  105.0 0.2 fusion.62
  105.2 0.4 fusion.64
  105.6 1.2 dynamic_slice.51
  106.9 0.6 iota_compare_fusion.3
  107.4 0.3 fusion.61
  107.7 0.2 fusion.62
  107.9 0.4 fusion.64
  108.3 0.7 multiply_add_fusion
  109.0 1.0 convolution_multiply_fusion.2
  110.0 1.2 fusion.23
  111.2 0.7 reshape.33
  112.0 38.6 %all-gather.2.cloned.1.call-done = bf16[1024,512]{1,0:T(8,128)(2,1)} async-done(((bf16[128,512]{1,0:T(8,128)(2,1)}), bf16[1024,512]{1,0:T(8,128)(2,1)}) %all-gather.2.cloned.1.call-update) | async-done | bytes 1048592 | tf_op jit(solution)/shard_map/all_gather | solution.py:100
  150.6 4.4 %fusion.41 = f32[1024,1024]{1,0:T(8,128)} fusion(bf16[1024,512]{1,0:T(8,128)(2,1)} %all-gather.2.cloned.1.call-done, bf16[512,1024]{1,0:T(8,128)(2,1)S(1)} %copy-done), kind=kOutput, calls=%fused_computation.62 | convolution fusion | flops 1073741824 | bytes 6291456 | tf_op jit(solution)/shard_map/dot_general | solution.py:102
  155.0 43.4 %reduce-scatter.2.cloned.1.call-done = f32[256,1024]{1,0:T(8,128)} async-done(((f32[1024,1024]{1,0:T(8,128)}), f32[256,1024]{1,0:T(8,128)}) %reduce-scatter.2.cloned.1.call-update) | async-done | bytes 1048592 | tf_op jit(solution)/shard_map/reduce_scatter | solution.py:101
  198.4 2.1 %convert_element_type.20 = bf16[256,1024]{1,0:T(8,128)(2,1)} convert(f32[256,1024]{1,0:T(8,128)} %reduce-scatter.2.cloned.1.call-done) | non-fusion elementwise | flops 262144 | bytes 1572864 | tf_op jit(solution)/shard_map/convert_element_type | solution.py:107
  (25 shorter events, 0.5 us)
Async XLA Ops:
  6.5 144.0 %copy-start = (bf16[512,1024]{1,0:T(8,128)(2,1)S(1)}, bf16[512,1024]{1,0:T(8,128)(2,1)}, u32[]{:S(2)}) copy-start(bf16[512,1024]{1,0:T(8,128)(2,1)} %param.13) | copy-start | bytes 3145732
  6.5 144.0 %all-gather.2.cloned.1.call-start = ((), (), s32[]{:S(2)}) async-start(), calls=%async_computation.1 | async-start | bytes 1179648 | tf_op jit(solution)/shard_map/all_gather | solution.py:100
  6.5 2.9 %collective-permute-start.1 = (bf16[128,128]{1,0:T(8,128)(2,1)}, bf16[128,128]{1,0:T(8,128)(2,1)S(1)}, u32[]{:S(2)}, u32[]{:S(2)}) collective-permute-start(bf16[128,128]{1,0:T(8,128)(2,1)} %param.9), channel_id=1, source_target_pairs={{0,1},{1,0},{2,3},{3,2},{4,5},{5,4},{6,7},{7,6},{8,9},{9,8},{10,11... | collective-permute-start | bytes 98312 | tf_op jit(solution)/shard_map/ppermute | solution.py:11
  7.0 14.5 %collective-permute-start = (bf16[1,384,128]{2,1,0:T(8,128)(2,1)}, bf16[1,384,128]{2,1,0:T(8,128)(2,1)S(1)}, u32[]{:S(2)}, u32[]{:S(2)}) collective-permute-start(bf16[1,384,128]{2,1,0:T(8,128)(2,1)} %param.10), channel_id=1, source_target_pairs={{0,1},{1,0},{2,3},{3,2},{4,5},{5,4},{6,7},{7,6},{8,9},{9,8},{10,11... | collective-permute-start | bytes 294920 | tf_op jit(solution)/shard_map/ppermute | solution.py:11
  10.9 9.8 %collective-permute-start.2 = (bf16[128,128]{1,0:T(8,128)(2,1)S(1)}, bf16[128,128]{1,0:T(8,128)(2,1)S(1)}, u32[]{:S(2)}, u32[]{:S(2)}) collective-permute-start(bf16[128,128]{1,0:T(8,128)(2,1)S(1)} %get-tuple-element.222), channel_id=1, source_target_pairs={{0,4},{4,8},{8,12},{12,16},{16,20},{20,24},{24,28},{1,5},{5,9},{9,... | collective-permute-start | bytes 98312 | tf_op jit(solution)/shard_map/ppermute | solution.py:17
  15.7 93.3 %collective-permute-start.3 = (bf16[128,128]{1,0:T(8,128)(2,1)}, bf16[128,128]{1,0:T(8,128)(2,1)}, u32[]{:S(2)}, u32[]{:S(2)}) collective-permute-start(bf16[128,128]{1,0:T(8,128)(2,1)} %get-tuple-element.223), channel_id=1, source_target_pairs={{0,4},{4,8},{8,12},{12,16},{16,20},{20,24},{24,28},{1,5},{5,9},{9,... | collective-permute-start | bytes 98312 | tf_op jit(solution)/shard_map/ppermute | solution.py:17
  111.9 86.5 %reduce-scatter.2.cloned.1.call-start = ((), (), s32[]{:S(2)}) async-start(), calls=%async_computation.2 | async-start | bytes 5242880 | tf_op jit(solution)/shard_map/reduce_scatter | solution.py:101
Sparse Core Ops, SparseCore 0:
  112.1 38.4 all-gather.1
  155.1 43.2 reduce-scatter.1
where the time goes:
time: 208 us; the launch traced here: 207 us
  waiting for transfers between devices  82 us (39%)
  blocking collectives  64.3 us (31%)
  between operations  13.6 us (7%)
  other arithmetic  13.1 us (6%)
  matrix products  12.6 us (6%)
  local copies, waits for them, and re-layouts  12 us (6%)
  starting transfers between devices  9.46 us (5%)
    reduce_scatter x1, waiting for transfers between devices, body(): lax.psum_scatter(jnp.dot(gathered, out_weight, preferred_element_type=jnp...  43.4 us
    all_gather x1, waiting for transfers between devices, body(): gathered = lax.all_gather(attention, 'doc', axis=0, tiled=True)  38.6 us
    all_gather x1, blocking collectives, body(): key_docs = lax.all_gather(doc_keys, 'doc', axis=0, tiled=True)  32.1 us
    all_gather x1, blocking collectives, body(): value_docs = lax.all_gather(doc_values, 'doc', axis=0, tiled=True)  32.1 us
    dynamic_slice x8, local copies, waits for them, and re-layouts, attend_doc(): length = lax.dynamic_index_in_dim(doc_lengths, doc_step, 0, keepdims=False)  9.87 us
    ppermute x2, starting transfers between devices, passed_along(): lax.ppermute(value, axis, [(source, source + steps) for source in range(i...  8.91 us
    dot_general x10, matrix products, block_stats(): jnp.dot(weights.astype(jnp.bfloat16), value_block, preferred_element_type...  5.52 us
    lt x8, other arithmetic, attend_doc(): visible = (slot_index < length)[None, :]  4.5 us
  transfers between devices with their start and end apart: 6, of which 2 were waited for; matrix products, arithmetic and copies ran while one was open for 14% of the time, Pallas kernels for 0%

commit v1 on v0

--- a/solution.py
+++ b/solution.py
@@ -5,6 +5,9 @@
 from jax.sharding import PartitionSpec as P
 
 masked_score = -1e30
+digits_produce = lambda z, t0, dev_axis: jnp.split(
+    lax.all_gather(jnp.concatenate([z, t0], axis=1), dev_axis, axis=0, tiled=True), [z.shape[1]], 1
+)
 
 
 def swapped(array, axis, stride):
@@ -63,8 +66,7 @@
     )
     partner_doc, partner_tgt = swapped((doc_kv, target_kv), "head", 0)
     doc_keys, doc_values = arrange(doc_kv, partner_doc)
-    key_docs = lax.all_gather(doc_keys, "doc", axis=0, tiled=True)
-    value_docs = lax.all_gather(doc_values, "doc", axis=0, tiled=True)
+    key_docs, value_docs = digits_produce(doc_keys, doc_values, dev_axis="doc")
     slot_index = jnp.arange(key_docs.shape[1], dtype=jnp.int32)
 
     def attend_doc(doc_step, running):

time: 208 us -> 181 us (0.87)
  blocking collectives: 64.3 us -> 0 us
  waiting for transfers between devices: 82 us -> 116 us
    all_gather x2 -> x0, blocking collectives: 64.3 us -> none  [the longest x1 32.1 us: body(): key_docs = lax.all_gather(doc_keys, 'doc', axis=0, tiled=True)]
    all_gather x0 -> x1, waiting for transfers between devices: none -> 32.4 us  [lax.all_gather(jnp.concatenate([z, t0], axis=1), dev_axis, axis=0, tiled=...]
  transfers between devices with their start and end apart: 6 -> 7, of which waited for: 2 -> 4; matrix products, arithmetic and copies ran while one was open for 14% -> 17% of each run, Pallas kernels for 0% -> 0%
where the time goes in v1:
time: 181 us; the launch traced here: 180 us
  waiting for transfers between devices  116 us (64%)
  other arithmetic  14.6 us (8%)
  local copies, waits for them, and re-layouts  13.6 us (8%)
  between operations  13.2 us (7%)
  matrix products  12.6 us (7%)
  starting transfers between devices  9.57 us (5%)
    reduce_scatter x1, waiting for transfers between devices, body(): lax.psum_scatter(jnp.dot(gathered, out_weight, preferred_element_type=jnp...  43.4 us
    all_gather x1, waiting for transfers between devices, body(): gathered = lax.all_gather(attention, 'doc', axis=0, tiled=True)  39.1 us
    all_gather x1, waiting for transfers between devices, lax.all_gather(jnp.concatenate([z, t0], axis=1), dev_axis, axis=0, tiled=...  32.4 us
    dynamic_slice x8, local copies, waits for them, and re-layouts, attend_doc(): length = lax.dynamic_index_in_dim(doc_lengths, doc_step, 0, keepdims=False)  9.94 us
    ppermute x2, starting transfers between devices, passed_along(): lax.ppermute(value, axis, [(source, source + steps) for source in range(i...  8.61 us
    dot_general x10, matrix products, block_stats(): jnp.dot(weights.astype(jnp.bfloat16), value_block, preferred_element_type...  5.52 us
    lt x8, other arithmetic, attend_doc(): visible = (slot_index < length)[None, :]  5.19 us
    dot_general x1, matrix products, body(): jnp.dot(gathered, out_weight, preferred_element_type=jnp.float32)  4.41 us
  transfers between devices with their start and end apart: 7, of which 4 were waited for; matrix products, arithmetic and copies ran while one was open for 17% of the time, Pallas kernels for 0%

profile of v1, /device:TPU:0, one launch (start us, length us, event | category | flops | bytes accessed | tf_op | source)
XLA Modules:
  0.0 180.0 jit_solution(3824269680605662698)
XLA Ops:
  6.5 0.5 collective-permute-start
  7.0 1.2 collective-permute-done
  8.1 0.9 broadcast_select_fusion.1
  9.1 0.7 pad_maximum_fusion
  9.8 0.4 collective-permute-start.1
  10.2 0.8 fusion.39
  11.7 1.0 reshape.30
  12.7 1.4 broadcast_select_fusion.3
  14.0 4.6 %collective-permute-start.2 = (bf16[128,128]{1,0:T(8,128)(2,1)S(1)}, bf16[128,128]{1,0:T(8,128)(2,1)S(1)}, u32[]{:S(2)}, u32[]{:S(2)}) collective-permute-start(bf16[128,128]{1,0:T(8,128)(2,1)S(1)} %get-tuple-element.224), channel_id=1, source_target_pairs={{0,4},{4,8},{8,12},{12,16},{16,20},{20,24},{24,28},{1,5},{5,9},{9,... | collective-permute-start | bytes 98312 | tf_op jit(solution)/shard_map/ppermute | solution.py:20
  18.6 4.0 %collective-permute-start.3 = (bf16[128,128]{1,0:T(8,128)(2,1)}, bf16[128,128]{1,0:T(8,128)(2,1)}, u32[]{:S(2)}, u32[]{:S(2)}) collective-permute-start(bf16[128,128]{1,0:T(8,128)(2,1)} %get-tuple-element.225), channel_id=1, source_target_pairs={{0,4},{4,8},{8,12},{12,16},{16,20},{20,24},{24,28},{1,5},{5,9},{9,... | collective-permute-start | bytes 98312 | tf_op jit(solution)/shard_map/ppermute | solution.py:20
  22.7 0.2 fusion.41
  22.9 0.7 fusion.24
  23.5 0.2 fusion.40
  23.7 0.6 fusion.26
  24.4 32.4 %all-gather.3.cloned.1.call-done = bf16[8,768,128]{2,1,0:T(8,128)(2,1)} async-done(((bf16[1,768,128]{2,1,0:T(8,128)(2,1)}), bf16[8,768,128]{2,1,0:T(8,128)(2,1)}) %all-gather.3.cloned.1.call-update) | async-done | bytes 1572880 | tf_op jit(solution)/shard_map/all_gather | solution.py:9
  56.8 1.5 fusion.38
  58.3 22.4 %while.18 = (s32[]{:T(128)}, f32[512]{0:T(512)S(1)}, f32[512]{0:T(512)S(1)}, f32[512,128]{1,0:T(8,128)S(1)}, s32[8]{0:T(128)}, /*index=5*/bf16[8,384,128]{2,1,0:...) while((s32[]{:T(128)}, f32[512]{0:T(512)S(1)}, ...), condition=%wide.region_3.4_spmd.clone, body=%wide.region_0.3_spmd.clone.sunk | while | flops 102305152 | bytes 3240976 | solution.py:79
  58.3 1.2 dynamic_slice.51
  59.6 0.6 iota_compare_fusion.3
  60.2 0.3 fusion.62
  60.5 0.2 fusion.63
  60.7 0.4 fusion.65
  61.1 1.2 dynamic_slice.51
  62.4 0.6 iota_compare_fusion.3
  63.0 0.3 fusion.62
  63.3 0.2 fusion.63
  63.5 0.4 fusion.65
  63.9 1.2 dynamic_slice.51
  65.2 0.6 iota_compare_fusion.3
  65.8 0.3 fusion.62
  66.1 0.2 fusion.63
  66.3 0.4 fusion.65
  66.8 1.2 dynamic_slice.51
  68.0 0.6 iota_compare_fusion.3
  68.7 0.3 fusion.62
  68.9 0.2 fusion.63
  69.1 0.4 fusion.65
  69.6 1.2 dynamic_slice.51
  70.8 0.6 iota_compare_fusion.3
  71.5 0.3 fusion.62
  71.7 0.2 fusion.63
  71.9 0.4 fusion.65
  72.4 1.2 dynamic_slice.51
  73.6 0.6 iota_compare_fusion.3
  74.3 0.3 fusion.62
  74.5 0.2 fusion.63
  74.7 0.4 fusion.65
  75.2 1.2 dynamic_slice.51
  76.4 0.6 iota_compare_fusion.3
  77.1 0.3 fusion.62
  77.4 0.2 fusion.63
  77.5 0.4 fusion.65
  78.0 1.2 dynamic_slice.51
  79.2 0.6 iota_compare_fusion.3
  79.9 0.3 fusion.62
  80.3 0.4 fusion.65
  80.8 0.7 multiply_add_fusion
  81.5 1.0 convolution_multiply_fusion.2
  82.5 1.2 fusion.23
  83.6 0.7 reshape.33
  84.5 39.1 %all-gather.5.cloned.1.call-done = bf16[1024,512]{1,0:T(8,128)(2,1)} async-done(((bf16[128,512]{1,0:T(8,128)(2,1)}), bf16[1024,512]{1,0:T(8,128)(2,1)}) %all-gather.5.cloned.1.call-update) | async-done | bytes 1048592 | tf_op jit(solution)/shard_map/all_gather | solution.py:102
  123.5 4.4 %fusion.42 = f32[1024,1024]{1,0:T(8,128)} fusion(bf16[1024,512]{1,0:T(8,128)(2,1)} %all-gather.5.cloned.1.call-done, bf16[512,1024]{1,0:T(8,128)(2,1)S(1)} %copy-done), kind=kOutput, calls=%fused_computation.64 | convolution fusion | flops 1073741824 | bytes 6291456 | tf_op jit(solution)/shard_map/dot_general | solution.py:104
  128.0 43.4 %reduce-scatter.2.cloned.1.call-done = f32[256,1024]{1,0:T(8,128)} async-done(((f32[1024,1024]{1,0:T(8,128)}), f32[256,1024]{1,0:T(8,128)}) %reduce-scatter.2.cloned.1.call-update) | async-done | bytes 1048592 | tf_op jit(solution)/shard_map/reduce_scatter | solution.py:103
  171.4 2.1 %convert_element_type.20 = bf16[256,1024]{1,0:T(8,128)(2,1)} convert(f32[256,1024]{1,0:T(8,128)} %reduce-scatter.2.cloned.1.call-done) | non-fusion elementwise | flops 262144 | bytes 1572864 | tf_op jit(solution)/shard_map/convert_element_type | solution.py:109
  (28 shorter events, 1.0 us)
Async XLA Ops:
  6.5 117.0 %copy-start = (bf16[512,1024]{1,0:T(8,128)(2,1)S(1)}, bf16[512,1024]{1,0:T(8,128)(2,1)}, u32[]{:S(2)}) copy-start(bf16[512,1024]{1,0:T(8,128)(2,1)} %param.13) | copy-start | bytes 3145732
  6.5 50.3 %all-gather.3.cloned.1.call-start = ((), (), s32[]{:S(2)}) async-start(), calls=%async_computation.1 | async-start | bytes 1769472 | tf_op jit(solution)/shard_map/all_gather | solution.py:9
  6.5 1.6 collective-permute-start
  9.8 113.7 %all-gather.5.cloned.1.call-start = ((), (), s32[]{:S(2)}) async-start(), calls=%async_computation.2 | async-start | bytes 1179648 | tf_op jit(solution)/shard_map/all_gather | solution.py:102
  9.8 2.8 %collective-permute-start.1 = (bf16[128,128]{1,0:T(8,128)(2,1)}, bf16[128,128]{1,0:T(8,128)(2,1)S(1)}, u32[]{:S(2)}, u32[]{:S(2)}) collective-permute-start(bf16[128,128]{1,0:T(8,128)(2,1)} %param.9), channel_id=1, source_target_pairs={{0,1},{1,0},{2,3},{3,2},{4,5},{5,4},{6,7},{7,6},{8,9},{9,8},{10,11... | collective-permute-start | bytes 98312 | tf_op jit(solution)/shard_map/ppermute | solution.py:14
  14.0 9.5 %collective-permute-start.2 = (bf16[128,128]{1,0:T(8,128)(2,1)S(1)}, bf16[128,128]{1,0:T(8,128)(2,1)S(1)}, u32[]{:S(2)}, u32[]{:S(2)}) collective-permute-start(bf16[128,128]{1,0:T(8,128)(2,1)S(1)} %get-tuple-element.224), channel_id=1, source_target_pairs={{0,4},{4,8},{8,12},{12,16},{16,20},{20,24},{24,28},{1,5},{5,9},{9,... | collective-permute-start | bytes 98312 | tf_op jit(solution)/shard_map/ppermute | solution.py:20
  18.6 62.8 %collective-permute-start.3 = (bf16[128,128]{1,0:T(8,128)(2,1)}, bf16[128,128]{1,0:T(8,128)(2,1)}, u32[]{:S(2)}, u32[]{:S(2)}) collective-permute-start(bf16[128,128]{1,0:T(8,128)(2,1)} %get-tuple-element.225), channel_id=1, source_target_pairs={{0,4},{4,8},{8,12},{12,16},{16,20},{20,24},{24,28},{1,5},{5,9},{9,... | collective-permute-start | bytes 98312 | tf_op jit(solution)/shard_map/ppermute | solution.py:20
  84.4 87.0 %reduce-scatter.2.cloned.1.call-start = ((), (), s32[]{:S(2)}) async-start(), calls=%async_computation.3 | async-start | bytes 5242880 | tf_op jit(solution)/shard_map/reduce_scatter | solution.py:103
Sparse Core Ops, SparseCore 0:
  9.9 46.8 all-gather.2
  84.5 38.9 all-gather.4
  128.1 43.2 reduce-scatter.1
